TPU v7x, 256 devices: a whole 4x4x8 slice. The times are simulated.
256 devices in a mesh: gen: 32 (over y, x, core), beam: 8 (over z).
Axes of the slice: x: 4, y: 4, z: 8, core: 2. Of those that a mesh axis runs over, the one named last changes fastest.
Arguments:
- gen_showers: bfloat16 [32768, 256], P('gen'), may hold values from -12 to 12
- beam_showers: bfloat16 [16384, 256], P('beam'), may hold values from -6 to 6
- embed_weight: bfloat16 [256, 128], replicated, may hold values from -0.375 to 0.375
- eps_roster: float32 [4], replicated, may hold values from 0.04 to 0.08
Outputs:
- gen_potential: float32 [32768], P('gen')
- beam_potential: float32 [16384], P('beam')
- weight_grad: float32 [256, 128], replicated
All inputs are finite; a program needn't handle non-finite values.
Results may differ from a plain program's by a relative error of at most 0.03.
Values sent between devices are 32-bit elements; how exact they have to be, the bound alone decides.
No kernel may reach another device: no remote copies, remote signals or barrier semaphores. Data moves between devices by JAX's collectives and lax.ppermute only.
A program may use at most 64 MiB of HBM per device.

v0:
```python
import math
import jax
import jax.numpy as jnp
from jax import lax
from jax.sharding import PartitionSpec as P

SWEEPS = 4


def embed(showers, weight):
    act = jnp.tanh(jnp.dot(showers, weight, preferred_element_type=jnp.float32))
    return (act, act.astype(jnp.bfloat16))


def tile_cost(gen_emb, beam_emb, gen_sq, beam_sq):
    cross = lax.dot_general(
        gen_emb, beam_emb, (((1,), (1,)), ((), ())), preferred_element_type=jnp.float32
    )
    return gen_sq[:, None] + beam_sq[None, :] - 2.0 * cross


def row_lse(scores):
    top = lax.pmax(jnp.max(scores, axis=1), "beam")
    total = lax.psum(jnp.sum(jnp.exp(scores - top[:, None]), axis=1), "beam")
    return top + jnp.log(total)


def col_lse(scores):
    top = lax.pmax(jnp.max(scores, axis=0), "gen")
    total = lax.psum(jnp.sum(jnp.exp(scores - top[None, :]), axis=0), "gen")
    return top + jnp.log(total)


def transpose_dot(left, right):
    return lax.dot_general(
        left.astype(jnp.float32),
        right,
        (((0,), (0,)), ((), ())),
        precision=lax.Precision.HIGHEST,
        preferred_element_type=jnp.float32,
    )


def on_device(gen_showers, beam_showers, embed_weight, eps_roster):
    gen_act, gen_emb = embed(gen_showers, embed_weight)
    beam_act, beam_emb = embed(beam_showers, embed_weight)
    gen_float = gen_emb.astype(jnp.float32)
    beam_float = beam_emb.astype(jnp.float32)
    gen_sq = jnp.sum(gen_float * gen_float, axis=1)
    beam_sq = jnp.sum(beam_float * beam_float, axis=1)
    rows = gen_emb.shape[0]
    columns = beam_emb.shape[0]
    log_beam = math.log(columns * lax.axis_size("beam"))
    log_gen = math.log(rows * lax.axis_size("gen"))
    beam_pot = jnp.zeros((columns,), jnp.float32)
    gen_pot = jnp.zeros((rows,), jnp.float32)
    for sweep in range(SWEEPS):
        temper = eps_roster[sweep]
        cost = tile_cost(gen_emb, beam_emb, gen_sq, beam_sq)
        gen_pot = temper * (log_beam - row_lse((beam_pot[None, :] - cost) / temper))
        cost = tile_cost(gen_emb, beam_emb, gen_sq, beam_sq)
        beam_pot = temper * (log_gen - col_lse((gen_pot[:, None] - cost) / temper))
    last = eps_roster[SWEEPS - 1]
    cost = tile_cost(gen_emb, beam_emb, gen_sq, beam_sq)
    mass = jnp.exp((gen_pot[:, None] + beam_pot[None, :] - cost) / last - log_beam)
    plan = mass.astype(jnp.bfloat16)
    gen_count = rows // lax.axis_size("beam")
    part = plan
    row_mass = jnp.sum(mass, axis=1)
    own = gen_float
    moved = jnp.dot(part, beam_emb, preferred_element_type=jnp.float32)
    grad_gen = lax.psum_scatter(
        2.0 * (row_mass[:, None] * own - moved), "beam", scatter_dimension=0, tiled=True
    )
    gen_start = lax.axis_index("beam") * gen_count
    act_rows = lax.dynamic_slice_in_dim(gen_act, gen_start, gen_count, 0)
    shower_rows = lax.dynamic_slice_in_dim(gen_showers, gen_start, gen_count, 0)
    beam_count = columns // lax.axis_size("gen")
    part = plan
    col_mass = jnp.sum(mass, axis=0)
    own = beam_float
    moved = lax.dot_general(
        part, gen_emb, (((0,), (0,)), ((), ())), preferred_element_type=jnp.float32
    )
    grad_beam = lax.psum_scatter(
        2.0 * (col_mass[:, None] * own - moved), "gen", scatter_dimension=0, tiled=True
    )
    beam_start = lax.axis_index("gen") * beam_count
    act_cols = lax.dynamic_slice_in_dim(beam_act, beam_start, beam_count, 0)
    shower_cols = lax.dynamic_slice_in_dim(beam_showers, beam_start, beam_count, 0)
    partial_grad = transpose_dot(shower_rows, grad_gen * (1.0 - act_rows * act_rows))
    partial_grad = partial_grad + transpose_dot(
        shower_cols, grad_beam * (1.0 - act_cols * act_cols)
    )
    weight_grad = lax.psum(partial_grad, ("gen", "beam"))
    return (gen_pot, beam_pot, weight_grad)


def solution(mesh):
    in_specs = (P("gen", None), P("beam", None), P(), P())
    out_specs = (P("gen"), P("beam"), P())
    return jax.shard_map(
        on_device, mesh=mesh, in_specs=in_specs, out_specs=out_specs, check_vma=False
    )
```

profile of v0, /device:TPU:8, one launch (start us, length us, event | category | flops | bytes accessed | tf_op | source)
XLA Modules:
  0.0 1114.6 jit_solution(14821040143072383777)
XLA Ops:
  11.4 5.3 fusion
  16.7 20.0 %pmax.56 = f32[1024]{0:T(1024)S(1)} all-reduce(f32[1024]{0:T(1024)S(1)} %get-tuple-element.16), channel_id=1, replica_groups=mesh['gen'=32,'beam'=8] {'beam'}, use_global_device_ids=true, to_apply=%region_3.0 | all-reduce | flops 1024 | bytes 8192 | tf_op jit(solution)/shard_map/pmax | solution.py:23
  41.8 14.2 %psum.63 = f32[1024]{0:T(1024)S(1)} all-reduce(f32[1024]{0:T(1024)S(1)} %exponential_reduce_fusion.7), channel_id=1, replica_groups=mesh['gen'=32,'beam'=8] {'beam'}, use_global_device_ids=true, to_apply=%region_5.0 | all-reduce | flops 1024 | bytes 8192 | tf_op jit(solution)/shard_map/psum | solution.py:24
  61.3 54.0 %pmax.57 = f32[2048]{0:T(1024)S(1)} all-reduce(f32[2048]{0:T(1024)S(1)} %fusion.15), channel_id=1, replica_groups=mesh['gen'=32,'beam'=8] {'gen'}, use_global_device_ids=true, to_apply=%region_7.0 | all-reduce | flops 2048 | bytes 16384 | tf_op jit(solution)/shard_map/pmax | solution.py:29
  115.4 5.2 exponential_reduce_fusion.6
  120.5 55.5 %psum.64 = f32[2048]{0:T(1024)S(1)} all-reduce(f32[2048]{0:T(1024)S(1)} %exponential_reduce_fusion.6), channel_id=1, replica_groups=mesh['gen'=32,'beam'=8] {'gen'}, use_global_device_ids=true, to_apply=%region_9.0 | all-reduce | flops 2048 | bytes 16384 | tf_op jit(solution)/shard_map/psum | solution.py:30
  181.5 16.2 %pmax.58 = f32[1024]{0:T(1024)S(1)} all-reduce(f32[1024]{0:T(1024)S(1)} %fusion.1), channel_id=1, replica_groups=mesh['gen'=32,'beam'=8] {'beam'}, use_global_device_ids=true, to_apply=%region_11.0 | all-reduce | flops 1024 | bytes 8192 | tf_op jit(solution)/shard_map/pmax | solution.py:23
  202.8 14.2 %psum.65 = f32[1024]{0:T(1024)S(1)} all-reduce(f32[1024]{0:T(1024)S(1)} %exponential_reduce_fusion.5), channel_id=1, replica_groups=mesh['gen'=32,'beam'=8] {'beam'}, use_global_device_ids=true, to_apply=%region_13.0 | all-reduce | flops 1024 | bytes 8192 | tf_op jit(solution)/shard_map/psum | solution.py:24
  222.1 63.7 %pmax.59 = f32[2048]{0:T(1024)S(1)} all-reduce(f32[2048]{0:T(1024)S(1)} %fusion.16), channel_id=1, replica_groups=mesh['gen'=32,'beam'=8] {'gen'}, use_global_device_ids=true, to_apply=%region_15.0 | all-reduce | flops 2048 | bytes 16384 | tf_op jit(solution)/shard_map/pmax | solution.py:29
  290.9 63.7 %psum.66 = f32[2048]{0:T(1024)S(1)} all-reduce(f32[2048]{0:T(1024)S(1)} %exponential_reduce_fusion.4), channel_id=1, replica_groups=mesh['gen'=32,'beam'=8] {'gen'}, use_global_device_ids=true, to_apply=%region_17.0 | all-reduce | flops 2048 | bytes 16384 | tf_op jit(solution)/shard_map/psum | solution.py:30
  360.1 16.2 %pmax.60 = f32[1024]{0:T(1024)S(1)} all-reduce(f32[1024]{0:T(1024)S(1)} %fusion.2), channel_id=1, replica_groups=mesh['gen'=32,'beam'=8] {'beam'}, use_global_device_ids=true, to_apply=%region_19.0 | all-reduce | flops 1024 | bytes 8192 | tf_op jit(solution)/shard_map/pmax | solution.py:23
  381.4 14.3 %psum.67 = f32[1024]{0:T(1024)S(1)} all-reduce(f32[1024]{0:T(1024)S(1)} %exponential_reduce_fusion.3), channel_id=1, replica_groups=mesh['gen'=32,'beam'=8] {'beam'}, use_global_device_ids=true, to_apply=%region_21.0 | all-reduce | flops 1024 | bytes 8192 | tf_op jit(solution)/shard_map/psum | solution.py:24
  401.1 63.7 %pmax.61 = f32[2048]{0:T(1024)S(1)} all-reduce(f32[2048]{0:T(1024)S(1)} %fusion.17), channel_id=1, replica_groups=mesh['gen'=32,'beam'=8] {'gen'}, use_global_device_ids=true, to_apply=%region_23.0 | all-reduce | flops 2048 | bytes 16384 | tf_op jit(solution)/shard_map/pmax | solution.py:29
  464.8 5.2 exponential_reduce_fusion.2
  470.0 63.7 %psum.68 = f32[2048]{0:T(1024)S(1)} all-reduce(f32[2048]{0:T(1024)S(1)} %exponential_reduce_fusion.2), channel_id=1, replica_groups=mesh['gen'=32,'beam'=8] {'gen'}, use_global_device_ids=true, to_apply=%region_25.0 | all-reduce | flops 2048 | bytes 16384 | tf_op jit(solution)/shard_map/psum | solution.py:30
  539.2 16.2 %pmax.62 = f32[1024]{0:T(1024)S(1)} all-reduce(f32[1024]{0:T(1024)S(1)} %fusion.3), channel_id=1, replica_groups=mesh['gen'=32,'beam'=8] {'beam'}, use_global_device_ids=true, to_apply=%region_27.0 | all-reduce | flops 1024 | bytes 8192 | tf_op jit(solution)/shard_map/pmax | solution.py:23
  560.5 14.2 %psum.69 = f32[1024]{0:T(1024)S(1)} all-reduce(f32[1024]{0:T(1024)S(1)} %exponential_reduce_fusion.1), channel_id=1, replica_groups=mesh['gen'=32,'beam'=8] {'beam'}, use_global_device_ids=true, to_apply=%region_29.0 | all-reduce | flops 1024 | bytes 8192 | tf_op jit(solution)/shard_map/psum | solution.py:24
  580.0 63.7 %pmax.63 = f32[2048]{0:T(1024)S(1)} all-reduce(f32[2048]{0:T(1024)S(1)} %fusion.18), channel_id=1, replica_groups=mesh['gen'=32,'beam'=8] {'gen'}, use_global_device_ids=true, to_apply=%region_31.0 | all-reduce | flops 2048 | bytes 16384 | tf_op jit(solution)/shard_map/pmax | solution.py:29
  643.7 5.2 exponential_reduce_fusion
  648.9 63.7 %psum.70 = f32[2048]{0:T(1024)S(1)} all-reduce(f32[2048]{0:T(1024)S(1)} %exponential_reduce_fusion), channel_id=1, replica_groups=mesh['gen'=32,'beam'=8] {'gen'}, use_global_device_ids=true, to_apply=%region_33.0 | all-reduce | flops 2048 | bytes 16384 | tf_op jit(solution)/shard_map/psum | solution.py:30
  713.3 5.7 fusion.37
  728.0 92.3 %reduce-scatter.5.cloned.1.call-done = f32[64,128]{1,0:T(8,128)} async-done(((f32[2048,128]{1,0:T(8,128)}), f32[64,128]{1,0:T(8,128)}) %reduce-scatter.5.cloned.1.call-update) | async-done | bytes 32784 | tf_op jit(solution)/shard_map/reduce_scatter | solution.py:85
  821.3 38.7 %reduce-scatter.3.cloned.1.call-done = f32[128,128]{0,1:T(8,128)} async-done(((f32[1024,128]{0,1:T(8,128)}), f32[128,128]{0,1:T(8,128)}) %reduce-scatter.3.cloned.1.call-update) | async-done | bytes 65552 | tf_op jit(solution)/shard_map/reduce_scatter | solution.py:72
  861.7 244.8 %all-reduce.2.cloned.1.call-done = f32[256,128]{1,0:T(8,128)} async-done(((f32[256,128]{1,0:T(8,128)}), f32[256,128]{1,0:T(8,128)}) %all-reduce.2.cloned.1.call-update) | async-done | bytes 131088 | tf_op jit(solution)/shard_map/psum | solution.py:95
  (42 shorter events, 81.4 us)
Async XLA Ops:
  7.2 1.5 copy-start
  7.2 813.0 %reduce-scatter.5.cloned.1.call-start = ((), (), s32[]{:S(2)}) async-start(), calls=%async_computation.3 | async-start | bytes 1081344 | tf_op jit(solution)/shard_map/reduce_scatter | solution.py:85
  575.4 137.9 %copy-start.2 = (f32[1024]{0:T(1024)}, f32[1024]{0:T(1024)S(1)}, u32[]{:S(2)}) copy-start(f32[1024]{0:T(1024)S(1)} %subtract_multiply_fusion.4) | copy-start | bytes 12292
  713.3 10.0 copy-start.3
  719.0 1.9 copy-start.1
  723.3 136.6 %reduce-scatter.3.cloned.1.call-start = ((), (), s32[]{:S(2)}) async-start(), calls=%async_computation.2 | async-start | bytes 589824 | tf_op jit(solution)/shard_map/reduce_scatter | solution.py:72
  727.9 378.6 %all-reduce.2.cloned.1.call-start = ((), (), s32[]{:S(2)}) async-start(), calls=%async_computation.4 | async-start | bytes 262144 | tf_op jit(solution)/shard_map/psum | solution.py:95
Sparse Core Ops, SparseCore 0:
  723.5 96.7 reduce-scatter.4
  822.9 36.9 reduce-scatter.2
  866.0 240.4 all-reduce.1
where the time goes:
time: 1120 us; the launch traced here: 1110 us
  blocking collectives  617 us (55%)
  waiting for transfers between devices  376 us (34%)
  other arithmetic  85 us (8%)
  matrix products  17.8 us (2%)
  between operations  14 us (1%)
    psum x4, blocking collectives, col_lse(): total = lax.psum(jnp.sum(jnp.exp(scores - top[None, :]), axis=0), 'gen')  247 us
    pmax x4, blocking collectives, col_lse(): top = lax.pmax(jnp.max(scores, axis=0), 'gen')  245 us
    psum x1, waiting for transfers between devices, on_device(): weight_grad = lax.psum(partial_grad, ('gen', 'beam'))  245 us
    reduce_scatter x1, waiting for transfers between devices, on_device(): lax.psum_scatter(2.0 * (col_mass[:, None] * own - moved), 'gen', scatter_...  92.3 us
    pmax x4, blocking collectives, row_lse(): top = lax.pmax(jnp.max(scores, axis=1), 'beam')  68.5 us
    psum x4, blocking collectives, row_lse(): total = lax.psum(jnp.sum(jnp.exp(scores - top[:, None]), axis=1), 'beam')  56.8 us
    reduce_scatter x1, waiting for transfers between devices, on_device(): lax.psum_scatter(2.0 * (row_mass[:, None] * own - moved), 'beam', scatter...  38.7 us
  transfers between devices with their start and end apart: 3, of which 3 were waited for; matrix products, arithmetic and copies ran while one was open for 0% of the time, Pallas kernels for 0%

commit v1 on v0

--- a/solution.py
+++ b/solution.py
@@ -27,7 +27,12 @@
 
 def col_lse(scores):
     top = lax.pmax(jnp.max(scores, axis=0), "gen")
-    total = lax.psum(jnp.sum(jnp.exp(scores - top[None, :]), axis=0), "gen")
+
+    def order_hubs(work_x, axis_name):
+        r_now = jnp.sum(lax.all_gather(work_x, axis_name), axis=0)
+        return r_now
+
+    total = order_hubs(jnp.sum(jnp.exp(scores - top[None, :]), axis=0), "gen")
     return top + jnp.log(total)
 
 

time: 1120 us -> 954 us (0.85)
  blocking collectives: 617 us -> 468 us
  waiting for transfers between devices: 376 us -> 361 us
    psum x4 -> x0, blocking collectives: 247 us -> none  [col_lse(): total = lax.psum(jnp.sum(jnp.exp(scores - top[None, :]), axis=0), 'gen')]
    all_gather x0 -> x4, blocking collectives: none -> 127 us  [order_hubs(): r_now = jnp.sum(lax.all_gather(work_x, axis_name), axis=0)]
    pmax x4, blocking collectives: 245 us -> 216 us  [col_lse(): top = lax.pmax(jnp.max(scores, axis=0), 'gen')]
    reduce_scatter x1, waiting for transfers between devices: 92.3 us -> 77.4 us  [on_device(): lax.psum_scatter(2.0 * (col_mass[:, None] * own - moved), 'gen', scatter_...]
  transfers between devices with their start and end apart: 3 -> 3, of which waited for: 3 -> 3; matrix products, arithmetic and copies ran while one was open for 0% -> 1% of each run, Pallas kernels for 0% -> 0%
where the time goes in v1:
time: 954 us; the launch traced here: 953 us
  blocking collectives  468 us (49%)
  waiting for transfers between devices  361 us (38%)
  other arithmetic  85.5 us (9%)
  matrix products  18.7 us (2%)
  between operations  14 us (1%)
    psum x1, waiting for transfers between devices, on_device(): weight_grad = lax.psum(partial_grad, ('gen', 'beam'))  245 us
    pmax x4, blocking collectives, col_lse(): top = lax.pmax(jnp.max(scores, axis=0), 'gen')  216 us
    all_gather x4, blocking collectives, order_hubs(): r_now = jnp.sum(lax.all_gather(work_x, axis_name), axis=0)  127 us
    reduce_scatter x1, waiting for transfers between devices, on_device(): lax.psum_scatter(2.0 * (col_mass[:, None] * own - moved), 'gen', scatter_...  77.4 us
    pmax x4, blocking collectives, row_lse(): top = lax.pmax(jnp.max(scores, axis=1), 'beam')  68.5 us
    psum x4, blocking collectives, row_lse(): total = lax.psum(jnp.sum(jnp.exp(scores - top[:, None]), axis=1), 'beam')  56.7 us
    reduce_scatter x1, waiting for transfers between devices, on_device(): lax.psum_scatter(2.0 * (row_mass[:, None] * own - moved), 'beam', scatter...  38.7 us
    reduce_sum x4, other arithmetic, col_lse(): total = order_hubs(jnp.sum(jnp.exp(scores - top[None, :]), axis=0), 'gen')  20.6 us
  transfers between devices with their start and end apart: 3, of which 3 were waited for; matrix products, arithmetic and copies ran while one was open for 1% of the time, Pallas kernels for 0%

profile of v1, /device:TPU:8, one launch (start us, length us, event | category | flops | bytes accessed | tf_op | source)
XLA Modules:
  0.0 952.5 jit_solution(18185014976563367344)
XLA Ops:
  12.2 5.3 fusion
  17.5 20.0 %pmax.56 = f32[1024]{0:T(1024)S(1)} all-reduce(f32[1024]{0:T(1024)S(1)} %get-tuple-element.16), channel_id=1, replica_groups=mesh['gen'=32,'beam'=8] {'beam'}, use_global_device_ids=true, to_apply=%region_3.0 | all-reduce | flops 1024 | bytes 8192 | tf_op jit(solution)/shard_map/pmax | solution.py:23
  42.7 14.2 %psum.35 = f32[1024]{0:T(1024)S(1)} all-reduce(f32[1024]{0:T(1024)S(1)} %exponential_reduce_fusion.7), channel_id=1, replica_groups=mesh['gen'=32,'beam'=8] {'beam'}, use_global_device_ids=true, to_apply=%region_5.0 | all-reduce | flops 1024 | bytes 8192 | tf_op jit(solution)/shard_map/psum | solution.py:24
  62.2 54.0 %pmax.57 = f32[2048]{0:T(1024)S(1)} all-reduce(f32[2048]{0:T(1024)S(1)} %fusion.15), channel_id=1, replica_groups=mesh['gen'=32,'beam'=8] {'gen'}, use_global_device_ids=true, to_apply=%region_7.0 | all-reduce | flops 2048 | bytes 16384 | tf_op jit(solution)/shard_map/pmax | solution.py:29
  116.2 5.2 exponential_reduce_fusion.6
  121.4 31.9 %all-gather = f32[65536]{0:T(1024)S(1)} all-gather(f32[2048]{0:T(1024)S(1)} %exponential_reduce_fusion.6), channel_id=2, replica_groups=mesh['gen'=32,'beam'=8] {'gen'}, dimensions={0}, use_global_device_ids=true | all-gather | bytes 270336 | tf_op jit(solution)/shard_map/all_gather | solution.py:32
  158.9 16.2 %pmax.58 = f32[1024]{0:T(1024)S(1)} all-reduce(f32[1024]{0:T(1024)S(1)} %fusion.1), channel_id=1, replica_groups=mesh['gen'=32,'beam'=8] {'beam'}, use_global_device_ids=true, to_apply=%region_11.0 | all-reduce | flops 1024 | bytes 8192 | tf_op jit(solution)/shard_map/pmax | solution.py:23
  180.2 14.2 %psum.36 = f32[1024]{0:T(1024)S(1)} all-reduce(f32[1024]{0:T(1024)S(1)} %exponential_reduce_fusion.5), channel_id=1, replica_groups=mesh['gen'=32,'beam'=8] {'beam'}, use_global_device_ids=true, to_apply=%region_13.0 | all-reduce | flops 1024 | bytes 8192 | tf_op jit(solution)/shard_map/psum | solution.py:24
  199.7 54.0 %pmax.59 = f32[2048]{0:T(1024)S(1)} all-reduce(f32[2048]{0:T(1024)S(1)} %fusion.16), channel_id=1, replica_groups=mesh['gen'=32,'beam'=8] {'gen'}, use_global_device_ids=true, to_apply=%region_15.0 | all-reduce | flops 2048 | bytes 16384 | tf_op jit(solution)/shard_map/pmax | solution.py:29
  258.9 31.7 %all-gather.1 = f32[65536]{0:T(1024)S(1)} all-gather(f32[2048]{0:T(1024)S(1)} %exponential_reduce_fusion.4), channel_id=3, replica_groups=mesh['gen'=32,'beam'=8] {'gen'}, dimensions={0}, use_global_device_ids=true | all-gather | bytes 270336 | tf_op jit(solution)/shard_map/all_gather | solution.py:32
  296.2 16.2 %pmax.60 = f32[1024]{0:T(1024)S(1)} all-reduce(f32[1024]{0:T(1024)S(1)} %fusion.2), channel_id=1, replica_groups=mesh['gen'=32,'beam'=8] {'beam'}, use_global_device_ids=true, to_apply=%region_19.0 | all-reduce | flops 1024 | bytes 8192 | tf_op jit(solution)/shard_map/pmax | solution.py:23
  317.5 14.2 %psum.37 = f32[1024]{0:T(1024)S(1)} all-reduce(f32[1024]{0:T(1024)S(1)} %exponential_reduce_fusion.3), channel_id=1, replica_groups=mesh['gen'=32,'beam'=8] {'beam'}, use_global_device_ids=true, to_apply=%region_21.0 | all-reduce | flops 1024 | bytes 8192 | tf_op jit(solution)/shard_map/psum | solution.py:24
  337.0 54.0 %pmax.61 = f32[2048]{0:T(1024)S(1)} all-reduce(f32[2048]{0:T(1024)S(1)} %fusion.17), channel_id=1, replica_groups=mesh['gen'=32,'beam'=8] {'gen'}, use_global_device_ids=true, to_apply=%region_23.0 | all-reduce | flops 2048 | bytes 16384 | tf_op jit(solution)/shard_map/pmax | solution.py:29
  391.0 5.2 exponential_reduce_fusion.2
  396.2 31.5 %all-gather.2 = f32[65536]{0:T(1024)S(1)} all-gather(f32[2048]{0:T(1024)S(1)} %exponential_reduce_fusion.2), channel_id=4, replica_groups=mesh['gen'=32,'beam'=8] {'gen'}, dimensions={0}, use_global_device_ids=true | all-gather | bytes 270336 | tf_op jit(solution)/shard_map/all_gather | solution.py:32
  433.4 16.2 %pmax.62 = f32[1024]{0:T(1024)S(1)} all-reduce(f32[1024]{0:T(1024)S(1)} %fusion.3), channel_id=1, replica_groups=mesh['gen'=32,'beam'=8] {'beam'}, use_global_device_ids=true, to_apply=%region_27.0 | all-reduce | flops 1024 | bytes 8192 | tf_op jit(solution)/shard_map/pmax | solution.py:23
  454.7 14.2 %psum.38 = f32[1024]{0:T(1024)S(1)} all-reduce(f32[1024]{0:T(1024)S(1)} %exponential_reduce_fusion.1), channel_id=1, replica_groups=mesh['gen'=32,'beam'=8] {'beam'}, use_global_device_ids=true, to_apply=%region_29.0 | all-reduce | flops 1024 | bytes 8192 | tf_op jit(solution)/shard_map/psum | solution.py:24
  474.2 54.0 %pmax.63 = f32[2048]{0:T(1024)S(1)} all-reduce(f32[2048]{0:T(1024)S(1)} %fusion.18), channel_id=1, replica_groups=mesh['gen'=32,'beam'=8] {'gen'}, use_global_device_ids=true, to_apply=%region_31.0 | all-reduce | flops 2048 | bytes 16384 | tf_op jit(solution)/shard_map/pmax | solution.py:29
  528.2 5.2 exponential_reduce_fusion
  533.4 31.7 %all-gather.3 = f32[65536]{0:T(1024)S(1)} all-gather(f32[2048]{0:T(1024)S(1)} %exponential_reduce_fusion), channel_id=5, replica_groups=mesh['gen'=32,'beam'=8] {'gen'}, dimensions={0}, use_global_device_ids=true | all-gather | bytes 270336 | tf_op jit(solution)/shard_map/all_gather | solution.py:32
  565.9 5.7 fusion.37
  580.6 77.4 %reduce-scatter.5.cloned.1.call-done = f32[64,128]{1,0:T(8,128)} async-done(((f32[2048,128]{1,0:T(8,128)}), f32[64,128]{1,0:T(8,128)}) %reduce-scatter.5.cloned.1.call-update) | async-done | bytes 32784 | tf_op jit(solution)/shard_map/reduce_scatter | solution.py:90
  659.1 38.7 %reduce-scatter.3.cloned.1.call-done = f32[128,128]{0,1:T(8,128)} async-done(((f32[1024,128]{0,1:T(8,128)}), f32[128,128]{0,1:T(8,128)}) %reduce-scatter.3.cloned.1.call-update) | async-done | bytes 65552 | tf_op jit(solution)/shard_map/reduce_scatter | solution.py:77
  699.6 244.9 %all-reduce.2.cloned.1.call-done = f32[256,128]{1,0:T(8,128)} async-done(((f32[256,128]{1,0:T(8,128)}), f32[256,128]{1,0:T(8,128)}) %all-reduce.2.cloned.1.call-update) | async-done | bytes 131088 | tf_op jit(solution)/shard_map/psum | solution.py:100
  (50 shorter events, 83.1 us)
Async XLA Ops:
  7.2 1.5 copy-start
  7.2 650.8 %reduce-scatter.5.cloned.1.call-start = ((), (), s32[]{:S(2)}) async-start(), calls=%async_computation.3 | async-start | bytes 1081344 | tf_op jit(solution)/shard_map/reduce_scatter | solution.py:90
  469.5 96.4 %copy-start.2 = (f32[1024]{0:T(1024)}, f32[1024]{0:T(1024)S(1)}, u32[]{:S(2)}) copy-start(f32[1024]{0:T(1024)S(1)} %subtract_multiply_fusion.4) | copy-start | bytes 12292
  565.9 10.0 %copy-start.3 = (f32[2048]{0:T(1024)}, f32[2048]{0:T(1024)S(1)}, u32[]{:S(2)}) copy-start(f32[2048]{0:T(1024)S(1)} %subtract_multiply_fusion) | copy-start | bytes 24580
  571.6 1.9 copy-start.1
  576.0 121.8 %reduce-scatter.3.cloned.1.call-start = ((), (), s32[]{:S(2)}) async-start(), calls=%async_computation.2 | async-start | bytes 589824 | tf_op jit(solution)/shard_map/reduce_scatter | solution.py:77
  580.6 363.9 %all-reduce.2.cloned.1.call-start = ((), (), s32[]{:S(2)}) async-start(), calls=%async_computation.4 | async-start | bytes 262144 | tf_op jit(solution)/shard_map/psum | solution.py:100
Sparse Core Ops, SparseCore 0:
  576.1 81.8 reduce-scatter.4
  660.7 36.9 reduce-scatter.2
  703.8 240.5 all-reduce.1
